TPU v7x, 512 devices: a whole 4x4x16 slice. The times are simulated.
512 devices in a mesh: row: 16 (over y, z_hi, core), col: 32 (over z_lo, x).
Axes of the slice: x: 4, y: 4, z: 16 (z_hi: 2, z_lo: 8; z = z_hi * 8 + z_lo), core: 2. Of those that a mesh axis runs over, the one named last changes fastest.
Arguments:
- blocks: bfloat16 [16, 32, 128, 128, 128], P('row', 'col'), may hold values from -0.115722656 to 0.115722656
- block_rows: int32 [16, 32, 128], P('row', 'col'), may hold values from 0 to 31
- block_cols: int32 [16, 32, 128], P('row', 'col'), may hold values from 0 to 63
- counts: int32 [16, 32], P('row', 'col'), may hold values from 1 to 128, as said below
- sketch: bfloat16 [1024, 48, 128], P(('row', 'col')), may hold values from -6 to 6
- adjoint_sketch: bfloat16 [1024, 48, 128], P(('col', 'row')), may hold values from -6 to 6
Outputs:
- image: float32 [1024, 48, 128], P(('col', 'row'))
- coimage: float32 [1024, 48, 128], P(('row', 'col'))
Inputs may be any that keep to these rules, and one draw needn't show every extreme that they name: `counts`: every draw has some tile with exactly 128 live slots; loads are skewed, the busiest some three times the mean.
All inputs are finite; a program needn't handle non-finite values.
Results may differ from a plain program's by a relative error of at most 0.0003.
Values may be sent and summed in bfloat16 or wider, within the bound.
A program may use at most 64 MiB of HBM per device.

v0:
```python
import jax
import jax.numpy as jnp
from jax import lax
from jax.sharding import PartitionSpec as P


def local(blocks, block_rows, block_cols, counts, sketch, adjoint_sketch):
    tile = blocks[0, 0]
    rows_k = block_rows[0, 0]
    cols_k = block_cols[0, 0]
    live_count = counts[0, 0]
    slots = tile.shape[0]
    owned = sketch.shape[0]
    live = (jnp.arange(slots, dtype=jnp.int32) < live_count).astype(jnp.float32)
    gathered = lax.all_gather(sketch, "col", axis=0, tiled=True)
    n_cols = gathered.shape[0]
    taken = gathered[cols_k]
    forward = jnp.einsum("kab,kcb->kca", tile, taken, preferred_element_type=jnp.float32)
    gathered_adj = lax.all_gather(adjoint_sketch, "row", axis=0, tiled=True)
    n_rows = gathered_adj.shape[0]
    given = gathered_adj[rows_k]
    backward = jnp.einsum("kab,kca->kcb", tile, given, preferred_element_type=jnp.float32)
    row_select = (rows_k[:, None] == jnp.arange(n_rows, dtype=jnp.int32)[None, :]).astype(
        jnp.float32
    ) * live[:, None]
    col_select = (cols_k[:, None] == jnp.arange(n_cols, dtype=jnp.int32)[None, :]).astype(
        jnp.float32
    ) * live[:, None]
    partial_rows = jnp.einsum("kr,kca->rca", row_select, forward, precision=lax.Precision.HIGHEST)
    summed_rows = lax.psum(partial_rows, "row")
    image = lax.dynamic_slice_in_dim(summed_rows, lax.axis_index("row") * owned, owned, 0)
    partial_cols = jnp.einsum("kr,kca->rca", col_select, backward, precision=lax.Precision.HIGHEST)
    summed_cols = lax.psum(partial_cols, "col")
    coimage = lax.dynamic_slice_in_dim(summed_cols, lax.axis_index("col") * owned, owned, 0)
    return (image, coimage)


def solution(mesh):
    in_specs = (
        P("row", "col", None, None, None),
        P("row", "col", None),
        P("row", "col", None),
        P("row", "col"),
        P(("row", "col"), None, None),
        P(("col", "row"), None, None),
    )
    out_specs = (P(("col", "row"), None, None), P(("row", "col"), None, None))
    return jax.shard_map(local, mesh=mesh, in_specs=in_specs, out_specs=out_specs, check_vma=False)
```

profile of v0, /device:TPU:24, one launch (start us, length us, event | category | flops | bytes accessed | tf_op | source)
XLA Modules:
  0.0 871.0 jit_solution(13089912056709050269)
XLA Ops:
  7.2 0.0 all-reduce.3.cloned.1.call-start
  7.9 129.3 %all_gather.6 = bf16[64,48,128]{2,1,0:T(8,128)(2,1)S(1)} all-gather(bf16[2,48,128]{2,1,0:T(8,128)(2,1)} %param.10), channel_id=1, replica_groups=mesh['row'=16,'col'=32] {'col'}, dimensions={0}, use_global_device_ids=true | all-gather | bytes 811008 | tf_op jit(solution)/shard_map/all_gather | solution.py:15
  137.2 0.7 fusion.18
  137.8 0.9 gather_fusion
  138.7 0.0 copy-start.1
  138.7 5.2 fusion.2
  143.9 0.0 copy-done.1
  143.9 3.5 fusion.6
  147.3 0.0 all-reduce.3.cloned.1.call-update
  147.4 0.0 all-reduce.5.cloned.1.call-start
  147.4 0.0 copy-done
  147.4 43.0 %all_gather.7 = bf16[32,48,128]{2,1,0:T(8,128)(2,1)S(1)} all-gather(bf16[2,48,128]{2,1,0:T(8,128)(2,1)S(1)} %copy-done), channel_id=1, replica_groups=mesh['row'=16,'col'=32] {'row'}, dimensions={0}, use_global_device_ids=true | all-gather | bytes 417792 | tf_op jit(solution)/shard_map/all_gather | solution.py:19
  190.5 0.9 gather_fusion.1
  191.3 0.0 copy-start.2
  191.3 3.4 fusion
  194.8 0.0 copy-done.2
  194.8 3.8 fusion.4
  198.6 0.0 all-reduce.5.cloned.1.call-update
  198.6 196.8 %all-reduce.3.cloned.1.call-done = f32[32,48,128]{2,0,1:T(8,128)} async-done(((f32[32,48,128]{2,0,1:T(8,128)}), f32[32,48,128]{2,0,1:T(8,128)}) %all-reduce.3.cloned.1.call-update) | async-done | bytes 786448 | tf_op jit(solution)/shard_map/psum | solution.py:30
  395.4 0.9 constant_dynamic-slice_fusion.1
  396.4 0.6 copy.10
  397.0 465.6 %all-reduce.5.cloned.1.call-done = f32[64,48,128]{2,0,1:T(8,128)} async-done(((f32[64,48,128]{2,0,1:T(8,128)}), f32[64,48,128]{2,0,1:T(8,128)}) %all-reduce.5.cloned.1.call-update) | async-done | bytes 1572880 | tf_op jit(solution)/shard_map/psum | solution.py:33
  862.6 0.9 constant_dynamic-slice_fusion
  863.6 0.6 copy.11
  (5 shorter events, 0.0 us)
Async XLA Ops:
  7.2 388.3 %all-reduce.3.cloned.1.call-start = ((), (), s32[]{:S(2)}) async-start(), calls=%async_computation | async-start | bytes 1572864 | tf_op jit(solution)/shard_map/psum | solution.py:30
  138.7 5.2 copy-start.1
  143.9 3.6 copy-start
  147.4 715.3 %all-reduce.5.cloned.1.call-start = ((), (), s32[]{:S(2)}) async-start(), calls=%async_computation.1 | async-start | bytes 3145728 | tf_op jit(solution)/shard_map/psum | solution.py:33
  191.3 3.5 copy-start.2
Sparse Core Ops, SparseCore 0:
  147.5 247.9 all-reduce.2
  398.6 463.9 all-reduce.4
where the time goes:
time: 871 us
  waiting for transfers between devices  662 us (76%)
  blocking collectives  172 us (20%)
  matrix products  15.9 us (2%)
  between operations  14.8 us (2%)
    psum x1, waiting for transfers between devices, local(): summed_cols = lax.psum(partial_cols, 'col')  466 us
    psum x1, waiting for transfers between devices, local(): summed_rows = lax.psum(partial_rows, 'row')  197 us
    all_gather x1, blocking collectives, local(): gathered = lax.all_gather(sketch, 'col', axis=0, tiled=True)  129 us
    all_gather x1, blocking collectives, local(): gathered_adj = lax.all_gather(adjoint_sketch, 'row', axis=0, tiled=True)  43 us
  transfers between devices with their start and end apart: 2, of which 2 were waited for; matrix products, arithmetic and copies ran while one was open for 1% of the time, Pallas kernels for 0%

commit v1 on v0

v1 whole, which is shorter than its diff:
```python
import jax
import jax.numpy as jnp
from jax import lax
from jax.experimental import pallas as pl
from jax.experimental.pallas import tpu as pltpu
from jax.sharding import PartitionSpec as P

SLOTS = 128
COLS = 48
BLK = 128
NR = 32
NC = 64
T_ROW, T_COL, T_PREVR, T_PREVC, T_LASTR, T_LASTC, T_END = 0, 128, 256, 384, 512, 576, 640
XS = (1, 3, 2)
Z_NEAR = (1, 2, 3, 4, 5, 6, 7)
Z_FAR = (7, 6, 5, 4, 3, 2, 1)
NSEM = 128


def kernel(tab, blk_hbm, sk_hbm, ad_hbm, img_ref, coi_ref,
           w, ga, gs, accr, accc, sx, rx, sz, rz, sc, rc, sy, ry, sh, rh,
           lsem, wsem, ssem, rsem):
    r = lax.axis_index("row")
    c = lax.axis_index("col")
    y, zh, co = r // 4, (r // 2) % 2, r % 2
    zl, x = c // 4, c % 4

    def flip(v, m):
        out = 0
        bit = 1
        while bit < 8:
            b = (v // bit) % 2
            out = out + bit * ((1 - b) if (m & bit) else b)
            bit *= 2
        return out

    def peer(my=0, mzh=0, mco=0, mz=0, mx=0):
        y2, zh2, co2 = flip(y, my), flip(zh, mzh), flip(co, mco)
        zl2, x2 = flip(zl, mz), flip(x, mx)
        return (y2 * 4 + zh2 * 2 + co2, zl2 * 4 + x2)

    peers = ([dict(mzh=1), dict(mco=1)] + [dict(mz=m) for m in Z_FAR]
             + [dict(mx=m) for m in XS] + [dict(my=m) for m in XS])
    bar = pltpu.get_barrier_semaphore()
    for p in peers:
        pl.semaphore_signal(bar, inc=1, device_id=peer(**p), device_id_type=pl.DeviceIdType.MESH)

    parts = 4
    loads = []
    for i in range(parts):
        n = SLOTS // parts
        cp = pltpu.make_async_copy(blk_hbm.at[0, 0, pl.ds(i * n, n)], w.at[pl.ds(i * n, n)], wsem.at[i])
        cp.start()
        loads.append(cp)

    def ga_at(y_, zh_, co_, n=2):
        return pl.ds((co_ * 8 + y_ * 2 + zh_) * 2, n)

    def gs_at(zl_, x_):
        return pl.ds((zl_ * 4 + x_) * 2, 2)

    own_ad = pltpu.make_async_copy(ad_hbm, ga.at[ga_at(y, zh, co)], lsem.at[0])
    own_sk = pltpu.make_async_copy(sk_hbm, gs.at[gs_at(zl, x)], lsem.at[1])
    own_ad.start()
    own_sk.start()
    accr[0] = jnp.zeros((COLS, BLK), jnp.float32)
    accc[0] = jnp.zeros((COLS, BLK), jnp.float32)
    pl.semaphore_wait(bar, len(peers))

    count = [0]
    sent = []

    def send(src, dst, **p):
        i = count[0]
        count[0] += 1
        cp = pltpu.make_async_remote_copy(
            src_ref=src, dst_ref=dst, send_sem=ssem.at[i], recv_sem=rsem.at[i],
            device_id=peer(**p), device_id_type=pl.DeviceIdType.MESH)
        cp.start()
        sent.append(cp)
        return cp

    own_ga, own_gs = ga.at[ga_at(y, zh, co)], gs.at[gs_at(zl, x)]
    a_zh = send(ad_hbm, own_ga, mzh=1)
    s_z = {m: send(sk_hbm, own_gs, mz=m) for m in Z_FAR}
    a_y = {(m, 0): send(ad_hbm, own_ga, my=m) for m in XS}
    s_x = {(0, m): send(sk_hbm, own_gs, mx=m) for m in XS}

    def forward_z(m):
        s_z[m].wait_recv()
        ref = gs.at[gs_at(flip(zl, m), x)]
        for mx in XS:
            s_x[m, mx] = send(ref, ref, mx=mx)

    for m in (1, 2, 3):
        forward_z(m)
    a_zh.wait_recv()
    ref = ga.at[ga_at(y, flip(zh, 1), co)]
    for m in XS:
        a_y[m, 1] = send(ref, ref, my=m)
    own_ad.wait()
    ref = ga.at[ga_at(y, 0, co, 4)]
    a_co = {0: send(ref, ref, mco=1)}
    forward_z(4)
    forward_z(5)
    for m in XS:
        a_y[m, 0].wait_recv()
        a_y[m, 1].wait_recv()
        ref = ga.at[ga_at(flip(y, m), 0, co, 4)]
        a_co[m] = send(ref, ref, mco=1)
    forward_z(6)
    forward_z(7)
    for cp in loads:
        cp.wait()
    for m in (0,) + XS:
        a_co[m].wait_recv()

    def backward(k, carry):
        g = ga[tab[T_ROW + k]]
        prod = lax.dot_general(g, w[k], (((1,), (0,)), ((), ())), preferred_element_type=jnp.float32)
        accc[k + 1] = prod + accc[tab[T_PREVC + k]]
        return carry

    lax.fori_loop(0, SLOTS, backward, 0, unroll=8)

    def part_c(zl_, x_, s):
        return accc[tab[T_LASTC + (zl_ * 4 + x_) * 2 + s]]

    r_x = {}
    for mz in Z_FAR + (0,):
        for mx in XS:
            for s in range(2):
                sx[mx, mz, s] = part_c(flip(zl, mz), flip(x, mx), s)
            r_x[mx, mz] = send(sx.at[mx, mz], rx.at[mx, mz], mx=mx)

    own_sk.wait()
    for m in (0,) + Z_NEAR:
        for mx in XS:
            s_x[m, mx].wait_recv()

    def forward(k, carry):
        g = gs[tab[T_COL + k]]
        prod = lax.dot_general(g, w[k], (((1,), (1,)), ((), ())), preferred_element_type=jnp.float32)
        accr[k + 1] = prod + accr[tab[T_PREVR + k]]
        return carry

    r_z = {}

    def sum_x(mz, s):
        tot = part_c(flip(zl, mz), x, s)
        for mx in XS:
            tot = tot + rx[mx, mz, s]
        return tot

    def col_step(mz):
        for mx in XS:
            r_x[mx, mz].wait_recv()
        if mz:
            for s in range(2):
                sz[mz, s] = sum_x(mz, s)
            r_z[mz] = send(sz.at[mz], rz.at[mz], mz=mz)

    lax.fori_loop(0, SLOTS // 2, forward, 0, unroll=8)
    col_step(7)
    lax.fori_loop(SLOTS // 2, SLOTS, forward, 0, unroll=8)

    def part_r(y_, zh_, co_, s):
        return accr[tab[T_LASTR + (y_ * 4 + zh_ * 2 + co_) * 2 + s]]

    r_c = {}
    for m in XS + (0,):
        for h in range(2):
            for s in range(2):
                sc[m, h * 2 + s] = part_r(flip(y, m), flip(zh, h), flip(co, 1), s)
        r_c[m] = send(sc.at[m], rc.at[m], mco=1)
    col_step(6)
    r_y = {}
    for m in XS:
        r_c[m].wait_recv()
        for h in range(2):
            for s in range(2):
                sy[m, h * 2 + s] = part_r(flip(y, m), flip(zh, h), co, s) + rc[m, h * 2 + s]
        r_y[m] = send(sy.at[m], ry.at[m], my=m)
    col_step(5)
    col_step(4)
    r_c[0].wait_recv()
    for m in XS:
        r_y[m].wait_recv()

    def sum_y(h, s):
        tot = part_r(y, flip(zh, h), co, s) + rc[0, h * 2 + s]
        for m in XS:
            tot = tot + ry[m, h * 2 + s]
        return tot

    for s in range(2):
        sh[s] = sum_y(1, s)
    r_h = send(sh, rh, mzh=1)
    for mz in (3, 2, 1, 0):
        col_step(mz)
    r_h.wait_recv()
    for s in range(2):
        img_ref[s] = sum_y(0, s) + rh[s]
    for m in Z_NEAR:
        r_z[m].wait_recv()
    for s in range(2):
        tot = sum_x(0, s)
        for m in Z_NEAR:
            tot = tot + rz[m, s]
        coi_ref[s] = tot
    for cp in sent:
        cp.wait_send()


def table(rows_k, cols_k, count):
    slot = jnp.arange(SLOTS, dtype=jnp.int32)
    ends = jnp.arange(NC, dtype=jnp.int32)
    keys = jnp.stack([rows_k, cols_k])
    query = jnp.stack([jnp.concatenate([rows_k, ends]), jnp.concatenate([cols_k, ends])])
    limit = jnp.concatenate([slot, jnp.broadcast_to(count, (NC,))])
    hit = (keys[:, None, :] == query[:, :, None]) & (slot[None, None, :] < limit[None, :, None])
    last = jnp.max(jnp.where(hit, slot + 1, 0), axis=-1)
    s, q = rows_k % 2, rows_k // 2
    where_row = ((q % 2) * 8 + (q // 4) * 2 + (q // 2) % 2) * 2 + s
    return jnp.concatenate([where_row, cols_k, last[0, :SLOTS], last[1, :SLOTS], last[0, SLOTS:], last[1, SLOTS:]])


def local(blocks, block_rows, block_cols, counts, sketch, adjoint_sketch):
    tab = table(block_rows[0, 0], block_cols[0, 0], counts[0, 0])
    f32, bf16 = jnp.float32, jnp.bfloat16
    blk = (COLS, BLK)
    out = jax.ShapeDtypeStruct((2,) + blk, f32)
    return pl.pallas_call(
        kernel,
        out_shape=(out, out),
        in_specs=[
            pl.BlockSpec(memory_space=pltpu.SMEM),
            pl.BlockSpec(memory_space=pl.ANY),
            pl.BlockSpec(memory_space=pl.ANY),
            pl.BlockSpec(memory_space=pl.ANY),
        ],
        out_specs=(pl.BlockSpec(memory_space=pltpu.VMEM), pl.BlockSpec(memory_space=pltpu.VMEM)),
        scratch_shapes=[
            pltpu.VMEM((SLOTS, BLK, BLK), bf16),
            pltpu.VMEM((NR,) + blk, bf16),
            pltpu.VMEM((NC,) + blk, bf16),
            pltpu.VMEM((SLOTS + 1,) + blk, f32),
            pltpu.VMEM((SLOTS + 1,) + blk, f32),
            pltpu.VMEM((4, 8, 2) + blk, f32),
            pltpu.VMEM((4, 8, 2) + blk, f32),
            pltpu.VMEM((8, 2) + blk, f32),
            pltpu.VMEM((8, 2) + blk, f32),
            pltpu.VMEM((4, 4) + blk, f32),
            pltpu.VMEM((4, 4) + blk, f32),
            pltpu.VMEM((4, 4) + blk, f32),
            pltpu.VMEM((4, 4) + blk, f32),
            pltpu.VMEM((2,) + blk, f32),
            pltpu.VMEM((2,) + blk, f32),
            pltpu.SemaphoreType.DMA((2,)),
            pltpu.SemaphoreType.DMA((4,)),
            pltpu.SemaphoreType.DMA((NSEM,)),
            pltpu.SemaphoreType.DMA((NSEM,)),
        ],
        compiler_params=pltpu.CompilerParams(
            collective_id=0, has_side_effects=True, vmem_limit_bytes=48 * 1024 * 1024),
        cost_estimate=pl.CostEstimate(flops=2 * 201326592 * 2, bytes_accessed=4400000, transcendentals=0),
        name="flow",
    )(tab, blocks, sketch, adjoint_sketch)


def solution(mesh):
    in_specs = (
        P("row", "col", None, None, None),
        P("row", "col", None),
        P("row", "col", None),
        P("row", "col"),
        P(("row", "col"), None, None),
        P(("col", "row"), None, None),
    )
    out_specs = (P(("col", "row"), None, None), P(("row", "col"), None, None))
    return jax.shard_map(local, mesh=mesh, in_specs=in_specs, out_specs=out_specs, check_vma=False)
```

time: 871 us -> 78 us (0.09)
  the two profiles are of different devices: /device:TPU:24 before, /device:TPU:1 now
where the time goes in v1:
time: 78 us; the launch traced here: 77.7 us
  Pallas kernels  68.3 us (88%)
  local copies, waits for them, and re-layouts  5.66 us (7%)
  other arithmetic  2.39 us (3%)
  between operations  1.34 us (2%)
    pallas_call x1, Pallas kernels, local(): pl.pallas_call(kernel, out_shape=(out, out), in_specs=[pl.BlockSpec(memor...  68.3 us
    unnamed x8, local copies, waits for them, and re-layouts  4.9 us

profile of v1, /device:TPU:1, one launch (start us, length us, event | category | flops | bytes accessed | tf_op | source)
XLA Modules:
  0.0 77.7 jit_solution(4100254699084059073)
XLA Ops:
  1.3 0.7 fusion.1
  2.0 0.7 pad_add_fusion.3
  2.7 0.7 pad_add_fusion.2
  3.4 0.1 iota_compare_fusion
  3.5 0.2 select_reduce_fusion
  3.7 0.7 concatenate.15.tab
  4.5 0.0 copy-start
  4.5 2.2 %copy-done = bf16[1,1,128,128,128]{4,3,2,1,0:T(8,128)(2,1)S(1)} copy-done((bf16[1,1,128,128,128]{4,3,2,1,0:T(8,128)(2,1)S(1)}, bf16[1,1,128,128,128]{4,3,2,1,0:T(8,128)(2,1)}, u32[]{:S(2)}) %copy-start) | copy-done | bytes 4194328
  6.7 0.0 copy-start.1
  6.7 0.7 copy-done.1
  7.4 0.0 copy-start.2
  7.4 0.7 copy-done.2
  8.1 68.3 %flow.1 = (f32[2,48,128]{2,1,0:T(8,128)S(1)}, f32[2,48,128]{2,1,0:T(8,128)S(1)}) custom-call(s32[640]{0:T(1024)S(1)} %concatenate.15.tab, bf16[1,1,128,128,128]{4,3,2,1,0:T(8,128)(2,1)S(1)} %copy-done, bf16[2,48,128]{2,1,0:T(8,128)(2,1)S(1)} %copy-done.1, bf16[2,48,128]{2,1,0:T(8,128)(2,1)S(1)} %copy-done.2), custom_call_target="tpu_custom_call" | custom-call | flops 805306368 | bytes 4400000 | tf_op jit(solution)/shard_map/flow/pallas_call | solution.py:233
  76.4 0.6 copy.11
  77.1 0.6 copy.12
  (7 shorter events, 0.0 us)
Async XLA Ops:
  4.5 2.2 %copy-start = (bf16[1,1,128,128,128]{4,3,2,1,0:T(8,128)(2,1)S(1)}, bf16[1,1,128,128,128]{4,3,2,1,0:T(8,128)(2,1)}, u32[]{:S(2)}) copy-start(bf16[1,1,128,128,128]{4,3,2,1,0:T(8,128)(2,1)} %blk_hbm.1) | copy-start | bytes 12582916
  6.7 0.7 copy-start.1
  7.4 0.7 copy-start.2

commit v2 on v0

v2 whole, which is shorter than its diff:
```python
import jax
import jax.numpy as jnp
from jax import lax
from jax.experimental import pallas as pl
from jax.experimental.pallas import tpu as pltpu
from jax.sharding import PartitionSpec as P

SLOTS = 128
COLS = 48
BLK = 128
NR = 32
NC = 64
PREVR, PREVC, LASTR, LASTC = 0, 1, 2, 3
OTHERS = (1, 3, 2)
NSEM = 64
FULL = 32752.0
CODED2 = 2 * COLS + 16
CODED4 = 4 * COLS + 16


def encode(dst, vals):
    n = len(vals)
    row = lax.broadcasted_iota(jnp.int32, (16, BLK), 0)
    powers = jnp.zeros((16, BLK), jnp.int32)
    for i, v in enumerate(vals):
        most = jnp.maximum(jnp.max(jnp.abs(v), axis=0, keepdims=True), 1e-30)
        e = jnp.ceil(jnp.log2(most))
        whole = jnp.round(v * (jnp.exp2(-e) * FULL))
        dst[pl.ds(i * COLS, COLS)] = whole.astype(jnp.int32).astype(jnp.int16)
        powers = jnp.where(row == i, e.astype(jnp.int32), powers)
    dst[pl.ds(n * COLS, 16)] = powers.astype(jnp.int16)


def decode(src, n):
    powers = src[pl.ds(n * COLS, 16)].astype(jnp.int32).astype(jnp.float32)
    scale = jnp.exp2(powers) * (1.0 / FULL)
    return [src[pl.ds(i * COLS, COLS)].astype(jnp.int32).astype(jnp.float32) * scale[i:i + 1]
            for i in range(n)]


def flip(v, m):
    out = 0
    for bit in (1, 2, 4):
        b = (v // bit) % 2
        out = out + bit * ((1 - b) if (m & bit) else b)
    return out


def kernel(cnt, rows_hbm, cols_hbm, blk_hbm, sk_hbm, ad_hbm, out_ref,
           w, ga, gs, accr, accc, rows_s, cols_s, keys, wide, tabv, tab,
           sx, rx, sz, rz, sz2, rz2, sc, rc, sy, ry, sh, rh,
           lsem, wsem, ssem, rsem):
    r = lax.axis_index("row")
    c = lax.axis_index("col")
    y, zh, co = r // 4, (r // 2) % 2, r % 2
    zl, x = c // 4, c % 4

    def peer(my=0, mzh=0, mco=0, mz=0, mx=0):
        y2, zh2, co2 = flip(y, my), flip(zh, mzh), flip(co, mco)
        zl2, x2 = flip(zl, mz), flip(x, mx)
        return (y2 * 4 + zh2 * 2 + co2, zl2 * 4 + x2)

    peers = ([dict(mzh=1), dict(mz=4)] + [dict(mz=m) for m in OTHERS]
             + [dict(mx=m) for m in OTHERS] + [dict(my=m) for m in OTHERS] + [dict(mco=1)])
    bar = pltpu.get_barrier_semaphore()
    for p in peers:
        pl.semaphore_signal(bar, inc=1, device_id=peer(**p), device_id_type=pl.DeviceIdType.MESH)

    def ga_at(y_, zh_, co_, n=2):
        return pl.ds((co_ * 8 + y_ * 2 + zh_) * 2, n)

    def gs_at(zl_, x_, n=2):
        return pl.ds((x_ * 8 + zl_) * 2, n)

    def local_copy(src, dst, sem):
        cp = pltpu.make_async_copy(src, dst, sem)
        cp.start()
        return cp

    ids = [local_copy(rows_hbm, rows_s, lsem.at[2]),
           local_copy(cols_hbm, cols_s, lsem.at[3]),
           local_copy(rows_hbm, keys.at[0], lsem.at[4]),
           local_copy(cols_hbm, keys.at[1], lsem.at[5])]
    own_ad = local_copy(ad_hbm, ga.at[ga_at(y, zh, co)], lsem.at[0])
    own_sk = local_copy(sk_hbm, gs.at[gs_at(zl, x)], lsem.at[1])
    parts = 4
    loads = []
    for i in range(parts):
        n = SLOTS // parts
        loads.append(local_copy(blk_hbm.at[0, 0, pl.ds(i * n, n)], w.at[pl.ds(i * n, n)], wsem.at[i]))
    accr[0] = jnp.zeros((COLS, BLK), jnp.float32)
    accc[0] = jnp.zeros((COLS, BLK), jnp.float32)

    for cp in ids:
        cp.wait()

    def spread(j, carry):
        wide[0, pl.ds(j, 1)] = jnp.full((1, SLOTS), rows_s[0, j], jnp.int32)
        wide[1, pl.ds(j, 1)] = jnp.full((1, SLOTS), cols_s[0, j], jnp.int32)
        return carry

    lax.fori_loop(0, SLOTS, spread, 0, unroll=8)
    down = lax.broadcasted_iota(jnp.int32, (SLOTS, SLOTS), 0)
    across = lax.broadcasted_iota(jnp.int32, (SLOTS, SLOTS), 1)
    for i in range(2):
        same = (wide[i] == keys[i]) & (down < across)
        tabv[pl.ds(PREVR + i, 1)] = jnp.max(jnp.where(same, down + 1, 0), axis=0, keepdims=True)
        ends = (wide[i] == across) & (down < cnt[0, 0])
        tabv[pl.ds(LASTR + i, 1)] = jnp.max(jnp.where(ends, down + 1, 0), axis=0, keepdims=True)
    tab_copy = local_copy(tabv, tab, lsem.at[6])

    pl.semaphore_wait(bar, len(peers))

    count = [0]
    sent = []

    def send(src, dst, **p):
        i = count[0]
        count[0] += 1
        cp = pltpu.make_async_remote_copy(
            src_ref=src, dst_ref=dst, send_sem=ssem.at[i], recv_sem=rsem.at[i],
            device_id=peer(**p), device_id_type=pl.DeviceIdType.MESH)
        cp.start()
        sent.append(cp)
        return cp

    own_ga, own_gs = ga.at[ga_at(y, zh, co)], gs.at[gs_at(zl, x)]
    a_zh = send(ad_hbm, own_ga, mzh=1)
    s_4 = send(sk_hbm, own_gs, mz=4)
    s_z = [send(sk_hbm, own_gs, mz=m) for m in (3, 2, 1)]
    a_y = {(m, 0): send(ad_hbm, own_ga, my=m) for m in OTHERS}
    own_sk.wait()
    for cp in s_z:
        cp.wait_recv()
    quad = gs.at[gs_at(zl // 4 * 4, x, 8)]
    s_x = [send(quad, quad, mx=m) for m in OTHERS]
    s_4.wait_recv()
    ref = gs.at[gs_at(flip(zl, 4), x)]
    s_z4 = [send(ref, ref, mz=m) for m in (3, 2, 1)]
    own_ad.wait()
    a_zh.wait_recv()
    ref = ga.at[ga_at(y, flip(zh, 1), co)]
    for m in OTHERS:
        a_y[m, 1] = send(ref, ref, my=m)
    ref = ga.at[ga_at(y, 0, co, 4)]
    a_co = [send(ref, ref, mco=1)]
    for cp in s_z4:
        cp.wait_recv()
    quad = gs.at[gs_at(flip(zl, 4) // 4 * 4, x, 8)]
    s_x += [send(quad, quad, mx=m) for m in OTHERS]
    for m in OTHERS:
        a_y[m, 0].wait_recv()
        a_y[m, 1].wait_recv()
        ref = ga.at[ga_at(flip(y, m), 0, co, 4)]
        a_co.append(send(ref, ref, mco=1))
    tab_copy.wait()
    for cp in loads:
        cp.wait()
    for cp in a_co:
        cp.wait_recv()

    def backward(k, carry):
        q = rows_s[0, k]
        g = ga[(q // 2 % 2) * 16 + (q // 8) * 4 + (q // 4 % 2) * 2 + q % 2]
        prod = lax.dot_general(g, w[k], (((1,), (0,)), ((), ())), preferred_element_type=jnp.float32)
        accc[k + 1] = prod + accc[tab[PREVC, k]]
        return carry

    lax.fori_loop(0, SLOTS, backward, 0, unroll=8)

    def part_c(zl_, x_, s):
        return accc[tab[LASTC, (zl_ * 4 + x_) * 2 + s]]

    def both(m):
        return [(flip(zl, m ^ far), s) for far in (0, 4) for s in range(2)]

    r_x = {}
    for m in (1, 2, 3, 0):
        for mx in OTHERS:
            encode(sx.at[mx, m], [part_c(z_, flip(x, mx), s) for z_, s in both(m)])
            r_x[mx, m] = send(sx.at[mx, m], rx.at[mx, m], mx=mx)

    for cp in s_x:
        cp.wait_recv()

    def forward(k, carry):
        q = cols_s[0, k]
        g = gs[(q // 2 % 4) * 16 + (q // 8) * 2 + q % 2]
        prod = lax.dot_general(g, w[k], (((1,), (1,)), ((), ())), preferred_element_type=jnp.float32)
        accr[k + 1] = prod + accr[tab[PREVR, k]]
        return carry

    lax.fori_loop(0, SLOTS, forward, 0, unroll=8)

    def part_r(y_, zh_, co_, s):
        return accr[tab[LASTR, (y_ * 4 + zh_ * 2 + co_) * 2 + s]]

    pairs = [(h, s) for h in range(2) for s in range(2)]
    r_c = {}
    for m in OTHERS + (0,):
        for i, (h, s) in enumerate(pairs):
            sc[m, i] = part_r(flip(y, m), flip(zh, h), flip(co, 1), s)
        r_c[m] = send(sc.at[m], rc.at[m], mco=1)

    def sum_x(m):
        tot = [part_c(z_, x, s) for z_, s in both(m)]
        for mx in OTHERS:
            r_x[mx, m].wait_recv()
            tot = [a + b for a, b in zip(tot, decode(rx.at[mx, m], 4))]
        return tot

    r_z = {}

    def col_step(m):
        encode(sz.at[m], sum_x(m))
        r_z[m] = send(sz.at[m], rz.at[m], mz=m)

    col_step(1)
    r_y = {}
    for m in OTHERS:
        r_c[m].wait_recv()
        encode(sy.at[m], [part_r(flip(y, m), flip(zh, h), co, s) + rc[m, i] for i, (h, s) in enumerate(pairs)])
        r_y[m] = send(sy.at[m], ry.at[m], my=m)
    col_step(2)
    r_c[0].wait_recv()
    tot = [part_r(y, flip(zh, h), co, s) + rc[0, i] for i, (h, s) in enumerate(pairs)]
    for m in OTHERS:
        r_y[m].wait_recv()
        tot = [a + b for a, b in zip(tot, decode(ry.at[m], 4))]
    encode(sh, tot[2:])
    r_h = send(sh, rh, mzh=1)
    for s in range(2):
        out_ref[s] = tot[s]
    col_step(3)
    tot = sum_x(0)
    for m in OTHERS:
        r_z[m].wait_recv()
        tot = [a + b for a, b in zip(tot, decode(rz.at[m], 4))]
    encode(sz2, tot[2:])
    r_z2 = send(sz2, rz2, mz=4)
    for s in range(2):
        out_ref[2 + s] = tot[s]
    r_h.wait_recv()
    for s, v in enumerate(decode(rh, 2)):
        out_ref[s] += v
    r_z2.wait_recv()
    for s, v in enumerate(decode(rz2, 2)):
        out_ref[2 + s] += v
    for cp in sent:
        cp.wait_send()


def local(blocks, block_rows, block_cols, counts, sketch, adjoint_sketch):
    f32, bf16, i16, i32 = jnp.float32, jnp.bfloat16, jnp.int16, jnp.int32
    blk = (COLS, BLK)
    hbm = pl.BlockSpec(memory_space=pltpu.HBM)
    out = pl.pallas_call(
        kernel,
        out_shape=jax.ShapeDtypeStruct((4,) + blk, f32),
        in_specs=[pl.BlockSpec(memory_space=pltpu.SMEM), hbm, hbm, hbm, hbm, hbm],
        out_specs=pl.BlockSpec(memory_space=pltpu.VMEM),
        scratch_shapes=[
            pltpu.VMEM((SLOTS, BLK, BLK), bf16),
            pltpu.VMEM((NR,) + blk, bf16),
            pltpu.VMEM((NC,) + blk, bf16),
            pltpu.VMEM((SLOTS + 1,) + blk, f32),
            pltpu.VMEM((SLOTS + 1,) + blk, f32),
            pltpu.SMEM((1, SLOTS), i32),
            pltpu.SMEM((1, SLOTS), i32),
            pltpu.VMEM((2, 1, SLOTS), i32),
            pltpu.VMEM((2, SLOTS, SLOTS), i32),
            pltpu.VMEM((8, SLOTS), i32),
            pltpu.SMEM((8, SLOTS), i32),
            pltpu.VMEM((4, 4, CODED4, BLK), i16),
            pltpu.VMEM((4, 4, CODED4, BLK), i16),
            pltpu.VMEM((4, CODED4, BLK), i16),
            pltpu.VMEM((4, CODED4, BLK), i16),
            pltpu.VMEM((CODED2, BLK), i16),
            pltpu.VMEM((CODED2, BLK), i16),
            pltpu.VMEM((4, 4) + blk, f32),
            pltpu.VMEM((4, 4) + blk, f32),
            pltpu.VMEM((4, CODED4, BLK), i16),
            pltpu.VMEM((4, CODED4, BLK), i16),
            pltpu.VMEM((CODED2, BLK), i16),
            pltpu.VMEM((CODED2, BLK), i16),
            pltpu.SemaphoreType.DMA((7,)),
            pltpu.SemaphoreType.DMA((4,)),
            pltpu.SemaphoreType.DMA((NSEM,)),
            pltpu.SemaphoreType.DMA((NSEM,)),
        ],
        compiler_params=pltpu.CompilerParams(
            collective_id=0, has_side_effects=True, vmem_limit_bytes=62 * 1024 * 1024),
        cost_estimate=pl.CostEstimate(flops=2 * 201326592 * 2, bytes_accessed=4400000, transcendentals=0),
        name="flow",
    )(counts, block_rows[0], block_cols[0], blocks, sketch, adjoint_sketch)
    return out[:2], out[2:]


def solution(mesh):
    in_specs = (
        P("row", "col", None, None, None),
        P("row", "col", None),
        P("row", "col", None),
        P("row", "col"),
        P(("row", "col"), None, None),
        P(("col", "row"), None, None),
    )
    out_specs = (P(("col", "row"), None, None), P(("row", "col"), None, None))
    return jax.shard_map(local, mesh=mesh, in_specs=in_specs, out_specs=out_specs, check_vma=False)
```

time: 871 us -> 59.8 us (0.07)
  the two profiles are of different devices: /device:TPU:24 before, /device:TPU:1 now
where the time goes in v2:
time: 59.8 us; the launch traced here: 59.1 us
  Pallas kernels  56.4 us (94%)
  local copies, waits for them, and re-layouts  1.46 us (2%)
  between operations  1.28 us (2%)
    pallas_call x1, Pallas kernels, local(): pl.pallas_call(kernel, out_shape=jax.ShapeDtypeStruct((4,) + blk, f32), i...  56.4 us
    slice x1, local copies, waits for them, and re-layouts, local(): return (out[:2], out[2:])  1.46 us

profile of v2, /device:TPU:1, one launch (start us, length us, event | category | flops | bytes accessed | tf_op | source)
XLA Modules:
  0.0 59.1 jit_solution(2654965573815183153)
XLA Ops:
  1.3 56.4 %flow.1 = f32[4,48,128]{2,1,0:T(8,128)} custom-call(s32[1,1]{1,0:T(1,128)S(6)} %copy.8.cnt, s32[1,128]{1,0:T(1,128)} %bitcast.2, s32[1,128]{1,0:T(1,128)} %bitcast.3, bf16[1,1,128,128,128]{4,3,2,1,0:T(8,128)(2,1)} %blk_hbm.1, bf16[2,48,128]{2,1,0:T(8,128)(2,1)} %sk_hbm.1, bf16[2,48,128]{2,1,0:T(8,128)(2,1)} %ad_hbm.1), custom_call_target="tpu_custom_call" | custom-call | flops 805306368 | bytes 4400000 | tf_op jit(solution)/shard_map/flow/pallas_call | solution.py:257
  57.6 1.5 %fusion = (f32[2,48,128]{2,1,0:T(8,128)}, f32[2,48,128]{2,1,0:T(8,128)}) fusion(f32[4,48,128]{2,1,0:T(8,128)} %flow.1), kind=kLoop, calls=%fused_computation | loop fusion | bytes 196608 | tf_op jit(solution)/shard_map/slice | solution.py:296

commit v3 on v2

--- a/solution.py
+++ b/solution.py
@@ -77,12 +77,12 @@
         cp.start()
         return cp
 
+    own_ad = local_copy(ad_hbm, ga.at[ga_at(y, zh, co)], lsem.at[0])
+    own_sk = local_copy(sk_hbm, gs.at[gs_at(zl, x)], lsem.at[1])
     ids = [local_copy(rows_hbm, rows_s, lsem.at[2]),
            local_copy(cols_hbm, cols_s, lsem.at[3]),
            local_copy(rows_hbm, keys.at[0], lsem.at[4]),
            local_copy(cols_hbm, keys.at[1], lsem.at[5])]
-    own_ad = local_copy(ad_hbm, ga.at[ga_at(y, zh, co)], lsem.at[0])
-    own_sk = local_copy(sk_hbm, gs.at[gs_at(zl, x)], lsem.at[1])
     parts = 4
     loads = []
     for i in range(parts):
@@ -91,6 +91,28 @@
     accr[0] = jnp.zeros((COLS, BLK), jnp.float32)
     accc[0] = jnp.zeros((COLS, BLK), jnp.float32)
 
+    own_ad.wait()
+    own_sk.wait()
+    pl.semaphore_wait(bar, len(peers))
+
+    count = [0]
+    sent = []
+
+    def send(src, dst, **p):
+        i = count[0]
+        count[0] += 1
+        cp = pltpu.make_async_remote_copy(
+            src_ref=src, dst_ref=dst, send_sem=ssem.at[i], recv_sem=rsem.at[i],
+            device_id=peer(**p), device_id_type=pl.DeviceIdType.MESH)
+        cp.start()
+        sent.append(cp)
+        return cp
+
+    own_ga, own_gs = ga.at[ga_at(y, zh, co)], gs.at[gs_at(zl, x)]
+    a_zh = send(own_ga, own_ga, mzh=1)
+    s_4 = send(own_gs, own_gs, mz=4)
+    s_z = [send(own_gs, own_gs, mz=m) for m in (3, 2, 1)]
+    a_y = {(m, 0): send(own_ga, own_ga, my=m) for m in OTHERS}
     for cp in ids:
         cp.wait()
 
@@ -109,27 +131,6 @@
         tabv[pl.ds(LASTR + i, 1)] = jnp.max(jnp.where(ends, down + 1, 0), axis=0, keepdims=True)
     tab_copy = local_copy(tabv, tab, lsem.at[6])
 
-    pl.semaphore_wait(bar, len(peers))
-
-    count = [0]
-    sent = []
-
-    def send(src, dst, **p):
-        i = count[0]
-        count[0] += 1
-        cp = pltpu.make_async_remote_copy(
-            src_ref=src, dst_ref=dst, send_sem=ssem.at[i], recv_sem=rsem.at[i],
-            device_id=peer(**p), device_id_type=pl.DeviceIdType.MESH)
-        cp.start()
-        sent.append(cp)
-        return cp
-
-    own_ga, own_gs = ga.at[ga_at(y, zh, co)], gs.at[gs_at(zl, x)]
-    a_zh = send(ad_hbm, own_ga, mzh=1)
-    s_4 = send(sk_hbm, own_gs, mz=4)
-    s_z = [send(sk_hbm, own_gs, mz=m) for m in (3, 2, 1)]
-    a_y = {(m, 0): send(ad_hbm, own_ga, my=m) for m in OTHERS}
-    own_sk.wait()
     for cp in s_z:
         cp.wait_recv()
     quad = gs.at[gs_at(zl // 4 * 4, x, 8)]
@@ -137,7 +138,6 @@
     s_4.wait_recv()
     ref = gs.at[gs_at(flip(zl, 4), x)]
     s_z4 = [send(ref, ref, mz=m) for m in (3, 2, 1)]
-    own_ad.wait()
     a_zh.wait_recv()
     ref = ga.at[ga_at(y, flip(zh, 1), co)]
     for m in OTHERS:
@@ -159,14 +159,25 @@
     for cp in a_co:
         cp.wait_recv()
 
-    def backward(k, carry):
+    def product(panels, first, second, k, axis):
+        both = lax.dot_general(
+            jnp.concatenate([panels[first], panels[second]], axis=0),
+            jnp.concatenate([w[k], w[k + 1]], axis=1 - axis),
+            (((1,), (axis,)), ((), ())), preferred_element_type=jnp.float32)
+        return both[:COLS, :BLK], both[COLS:, BLK:]
+
+    def ga_of(k):
         q = rows_s[0, k]
-        g = ga[(q // 2 % 2) * 16 + (q // 8) * 4 + (q // 4 % 2) * 2 + q % 2]
-        prod = lax.dot_general(g, w[k], (((1,), (0,)), ((), ())), preferred_element_type=jnp.float32)
-        accc[k + 1] = prod + accc[tab[PREVC, k]]
+        return (q // 2 % 2) * 16 + (q // 8) * 4 + (q // 4 % 2) * 2 + q % 2
+
+    def backward(i, carry):
+        k = 2 * i
+        one, two = product(ga, ga_of(k), ga_of(k + 1), k, 0)
+        accc[k + 1] = one + accc[tab[PREVC, k]]
+        accc[k + 2] = two + accc[tab[PREVC, k + 1]]
         return carry
 
-    lax.fori_loop(0, SLOTS, backward, 0, unroll=8)
+    lax.fori_loop(0, SLOTS // 2, backward, 0, unroll=16)
 
     def part_c(zl_, x_, s):
         return accc[tab[LASTC, (zl_ * 4 + x_) * 2 + s]]
@@ -183,14 +194,18 @@
     for cp in s_x:
         cp.wait_recv()
 
-    def forward(k, carry):
+    def gs_of(k):
         q = cols_s[0, k]
-        g = gs[(q // 2 % 4) * 16 + (q // 8) * 2 + q % 2]
-        prod = lax.dot_general(g, w[k], (((1,), (1,)), ((), ())), preferred_element_type=jnp.float32)
-        accr[k + 1] = prod + accr[tab[PREVR, k]]
+        return (q // 2 % 4) * 16 + (q // 8) * 2 + q % 2
+
+    def forward(i, carry):
+        k = 2 * i
+        one, two = product(gs, gs_of(k), gs_of(k + 1), k, 1)
+        accr[k + 1] = one + accr[tab[PREVR, k]]
+        accr[k + 2] = two + accr[tab[PREVR, k + 1]]
         return carry
 
-    lax.fori_loop(0, SLOTS, forward, 0, unroll=8)
+    lax.fori_loop(0, SLOTS // 2, forward, 0, unroll=16)
 
     def part_r(y_, zh_, co_, s):
         return accr[tab[LASTR, (y_ * 4 + zh_ * 2 + co_) * 2 + s]]

time: 59.8 us -> 58.1 us (0.972)
  Pallas kernels: 56.4 us -> 55 us
    pallas_call x1, Pallas kernels: 56.4 us -> 55 us  [local(): pl.pallas_call(kernel, out_shape=jax.ShapeDtypeStruct((4,) + blk, f32), i...]
where the time goes in v3:
time: 58.1 us; the launch traced here: 57.7 us
  Pallas kernels  55 us (95%)
  local copies, waits for them, and re-layouts  1.46 us (3%)
  between operations  1.28 us (2%)
    pallas_call x1, Pallas kernels, local(): pl.pallas_call(kernel, out_shape=jax.ShapeDtypeStruct((4,) + blk, f32), i...  55 us
    slice x1, local copies, waits for them, and re-layouts, local(): return (out[:2], out[2:])  1.46 us

profile of v3, /device:TPU:1, one launch (start us, length us, event | category | flops | bytes accessed | tf_op | source)
XLA Modules:
  0.0 57.7 jit_solution(14873721286287719013)
XLA Ops:
  1.3 55.0 %flow.1 = f32[4,48,128]{2,1,0:T(8,128)} custom-call(s32[1,1]{1,0:T(1,128)S(6)} %copy.8.cnt, s32[1,128]{1,0:T(1,128)} %bitcast.2, s32[1,128]{1,0:T(1,128)} %bitcast.3, bf16[1,1,128,128,128]{4,3,2,1,0:T(8,128)(2,1)} %blk_hbm.1, bf16[2,48,128]{2,1,0:T(8,128)(2,1)} %sk_hbm.1, bf16[2,48,128]{2,1,0:T(8,128)(2,1)} %ad_hbm.1), custom_call_target="tpu_custom_call" | custom-call | flops 805306368 | bytes 4400000 | tf_op jit(solution)/shard_map/flow/pallas_call | solution.py:272
  56.3 1.5 %fusion = (f32[2,48,128]{2,1,0:T(8,128)}, f32[2,48,128]{2,1,0:T(8,128)}) fusion(f32[4,48,128]{2,1,0:T(8,128)} %flow.1), kind=kLoop, calls=%fused_computation | loop fusion | bytes 196608 | tf_op jit(solution)/shard_map/slice | solution.py:311

commit v4 on v3

--- a/solution.py
+++ b/solution.py
@@ -230,12 +230,12 @@
         encode(sz.at[m], sum_x(m))
         r_z[m] = send(sz.at[m], rz.at[m], mz=m)
 
-    col_step(1)
     r_y = {}
     for m in OTHERS:
         r_c[m].wait_recv()
         encode(sy.at[m], [part_r(flip(y, m), flip(zh, h), co, s) + rc[m, i] for i, (h, s) in enumerate(pairs)])
         r_y[m] = send(sy.at[m], ry.at[m], my=m)
+    col_step(1)
     col_step(2)
     r_c[0].wait_recv()
     tot = [part_r(y, flip(zh, h), co, s) + rc[0, i] for i, (h, s) in enumerate(pairs)]

time: 58.1 us -> 57.6 us (level)
  Pallas kernels: 55 us -> 54.3 us
    pallas_call x1, Pallas kernels: 55 us -> 54.3 us  [local(): pl.pallas_call(kernel, out_shape=jax.ShapeDtypeStruct((4,) + blk, f32), i...]
where the time goes in v4:
time: 57.6 us; the launch traced here: 57 us
  Pallas kernels  54.3 us (94%)
  local copies, waits for them, and re-layouts  1.46 us (3%)
  between operations  1.28 us (2%)
    pallas_call x1, Pallas kernels, local(): pl.pallas_call(kernel, out_shape=jax.ShapeDtypeStruct((4,) + blk, f32), i...  54.3 us
    slice x1, local copies, waits for them, and re-layouts, local(): return (out[:2], out[2:])  1.46 us

profile of v4, /device:TPU:1, one launch (start us, length us, event | category | flops | bytes accessed | tf_op | source)
XLA Modules:
  0.0 57.0 jit_solution(4957891400492704929)
XLA Ops:
  1.3 54.3 %flow.1 = f32[4,48,128]{2,1,0:T(8,128)} custom-call(s32[1,1]{1,0:T(1,128)S(6)} %copy.8.cnt, s32[1,128]{1,0:T(1,128)} %bitcast.2, s32[1,128]{1,0:T(1,128)} %bitcast.3, bf16[1,1,128,128,128]{4,3,2,1,0:T(8,128)(2,1)} %blk_hbm.1, bf16[2,48,128]{2,1,0:T(8,128)(2,1)} %sk_hbm.1, bf16[2,48,128]{2,1,0:T(8,128)(2,1)} %ad_hbm.1), custom_call_target="tpu_custom_call" | custom-call | flops 805306368 | bytes 4400000 | tf_op jit(solution)/shard_map/flow/pallas_call | solution.py:272
  55.6 1.5 %fusion = (f32[2,48,128]{2,1,0:T(8,128)}, f32[2,48,128]{2,1,0:T(8,128)}) fusion(f32[4,48,128]{2,1,0:T(8,128)} %flow.1), kind=kLoop, calls=%fused_computation | loop fusion | bytes 196608 | tf_op jit(solution)/shard_map/slice | solution.py:311
